TPU v7x, 32 devices: a whole 2x2x4 slice. The times are simulated.
32 devices in a mesh: groups: 2 (over y), tensor: 4 (over z), dp: 4 (over x, core).
Axes of the slice: x: 2, y: 2, z: 4, core: 2. Of those that a mesh axis runs over, the one named last changes fastest.
Arguments:
- acts: bfloat16 [8, 288, 4096], P(('groups', 'dp')), parts along dimension 0, may hold values from -6 to 6
- out_grads: bfloat16 [8, 288, 14336], P(('groups', 'dp'), None, 'tensor'), parts along dimension 0, may hold values from -0.29882812 to 0.29882812
- basis_in: bfloat16 [8192, 4096], P(('groups', 'dp'), 'tensor'), parts along dimension 0, may hold values from -0.09375 to 0.09375
- basis_out: bfloat16 [28672, 14336], P(('groups', 'dp'), 'tensor'), parts along dimension 0, may hold values from -0.046875 to 0.046875
- lengths: int32 [8], P(('groups', 'dp')), parts along dimension 0, may hold values from 96 to 288
Outputs:
- corrections: bfloat16 [28672, 4096], P(('groups', 'tensor'), 'dp'), parts along dimension 0
There are 2 independent parts, one for each index of `groups`. A program takes and returns all parts, laid end to end along the dimension named above; each array names one. Nothing has to cross between parts.
All inputs are finite; a program needn't handle non-finite values.
Results may differ from a plain program's by a relative error of at most 0.0085.
Values may be sent and summed in bfloat16 or wider, within the bound.
No kernel may reach another device: no remote copies, remote signals or barrier semaphores. Data moves between devices by JAX's collectives and lax.ppermute only.
A program may use at most 320 MiB of HBM per device.

v0:
```python
import functools

import jax
import jax.numpy as jnp
from jax import lax
from jax.experimental import pallas as pl
from jax.experimental.pallas import tpu as pltpu
from jax.sharding import PartitionSpec as P

F32 = jnp.float32
BF16 = jnp.bfloat16
MIN_LEN = 96
ALIGN = 16
TILE = 256
STEPS = 4


def square_kernel(start_ref, out_ref, in_ref, c_ref):
    total = None
    for n in range(in_ref.shape[0]):
        rows = pl.ds(pl.multiple_of(start_ref[n], ALIGN), in_ref.shape[1])
        proj = lax.dot_general(out_ref[rows, :], in_ref[n], (((0,), (0,)), ((), ())), preferred_element_type=F32)
        total = proj * proj if total is None else total + proj * proj
    c_ref[...] = total.astype(c_ref.dtype)


def squares(starts, out_proj, in_proj):
    tokens, cols = out_proj.shape
    n, seq, ins = in_proj.shape
    tile = cols
    for t in (512, 256, 128):
        if cols % t == 0:
            tile = t
            break
    return pl.pallas_call(
        square_kernel,
        grid_spec=pltpu.PrefetchScalarGridSpec(
            num_scalar_prefetch=1,
            grid=(cols // tile,),
            in_specs=[
                pl.BlockSpec((tokens, tile), lambda i, s: (0, i)),
                pl.BlockSpec((n, seq, ins), lambda i, s: (0, 0, 0)),
            ],
            out_specs=pl.BlockSpec((tile, ins), lambda i, s: (i, 0)),
        ),
        out_shape=jax.ShapeDtypeStruct((cols, ins), BF16),
        compiler_params=pltpu.CompilerParams(vmem_limit_bytes=60 * 2**20),
        cost_estimate=pl.CostEstimate(
            flops=2 * n * seq * cols * ins, bytes_accessed=2 * (n * seq * (cols + ins) + cols * ins), transcendentals=0
        ),
    )(starts, out_proj, in_proj)


def product_kernel(c_ref, mine_ref, other_ref, b_mine_ref, b_other_ref, given_ref, held_ref):
    i = pl.program_id(0)
    total = jnp.dot(mine_ref[...], b_mine_ref[...], preferred_element_type=F32)
    total = total + jnp.dot(other_ref[...], b_other_ref[...], preferred_element_type=F32)

    @pl.when(i < pl.num_programs(0) // 2)
    def _():
        given_ref[...] = total.astype(given_ref.dtype)

    @pl.when(i >= pl.num_programs(0) // 2)
    def _():
        held_ref[...] = total


def products(c, mine, other, basis):
    rows, depth = mine.shape
    cols = basis.shape[1] // 2
    tile = 896 if cols % 896 == 0 else TILE
    per = cols // tile
    at = lambda i, c: jnp.where(i < per, (1 - c[0]) * per + i, c[0] * per + i - per)
    return pl.pallas_call(
        product_kernel,
        grid_spec=pltpu.PrefetchScalarGridSpec(
            num_scalar_prefetch=1,
            grid=(2 * per,),
            in_specs=[
                pl.BlockSpec((rows, depth), lambda i, c: (0, 0)),
                pl.BlockSpec((rows, depth), lambda i, c: (0, 0)),
                pl.BlockSpec((depth, tile), lambda i, c: (c[0], at(i, c))),
                pl.BlockSpec((depth, tile), lambda i, c: (1 - c[0], at(i, c))),
            ],
            out_specs=[
                pl.BlockSpec((rows, tile), lambda i, c: (0, jnp.minimum(i, per - 1))),
                pl.BlockSpec((rows, tile), lambda i, c: (0, jnp.maximum(i - per, 0))),
            ],
        ),
        out_shape=[jax.ShapeDtypeStruct((rows, cols), BF16), jax.ShapeDtypeStruct((rows, cols), F32)],
        compiler_params=pltpu.CompilerParams(vmem_limit_bytes=36 * 2**20),
        cost_estimate=pl.CostEstimate(flops=1, bytes_accessed=1, transcendentals=0),
    )(c.reshape(1), mine, other, basis, basis)


def pieces_kernel(pairs, start_ref, c_ref, *refs):
    own, rest, in_ref, out_ref, held = refs[:pairs], refs[pairs : 2 * pairs], refs[-3], refs[-2], refs[-1]
    i = pl.program_id(0)
    u = own[0].shape[1]

    def fill(parts):
        for j, part in enumerate(parts):
            held[j * u : (j + 1) * u, :] = part[0]
            k = 2 * pairs - 1 - j
            held[k * u : (k + 1) * u, :] = part[1]

    @pl.when(i < pl.num_programs(0) // 2)
    def _():
        fill(own)

    @pl.when(i >= pl.num_programs(0) // 2)
    def _():
        fill(rest)

    total = None
    for n in range(in_ref.shape[0]):
        rows = pl.ds(pl.multiple_of(start_ref[n], ALIGN), in_ref.shape[1])
        proj = lax.dot_general(held[rows, :], in_ref[n], (((0,), (0,)), ((), ())), preferred_element_type=F32)
        total = proj * proj if total is None else total + proj * proj
    out_ref[...] = total.astype(out_ref.dtype)


def squares_of_pieces(starts, c, own, rest, wins):
    pairs = len(own)
    u, cols = own[0].shape[1:]
    n, seq, ins = wins.shape
    tile = TILE
    per = cols // tile
    at = lambda i, s, c: (jnp.where(i < per, c[0] * per + i, (1 - c[0]) * per + i - per), 0)
    return pl.pallas_call(
        functools.partial(pieces_kernel, pairs),
        grid_spec=pltpu.PrefetchScalarGridSpec(
            num_scalar_prefetch=2,
            grid=(2 * per,),
            in_specs=[pl.BlockSpec((2, u, tile), lambda i, s, c: (0, 0, jnp.minimum(i, per - 1)))] * pairs
            + [pl.BlockSpec((2, u, tile), lambda i, s, c: (0, 0, jnp.maximum(i - per, 0)))] * pairs
            + [pl.BlockSpec((n, seq, ins), lambda i, s, c: (0, 0, 0))],
            out_specs=pl.BlockSpec((tile, ins), at),
            scratch_shapes=[pltpu.VMEM((2 * pairs * u, tile), BF16)],
        ),
        out_shape=jax.ShapeDtypeStruct((2 * cols, ins), BF16),
        compiler_params=pltpu.CompilerParams(vmem_limit_bytes=40 * 2**20),
        cost_estimate=pl.CostEstimate(flops=1, bytes_accessed=1, transcendentals=0),
    )(starts, c.reshape(1), *own, *rest, wins)


def swap_dp(x, k, n_dp):
    return lax.ppermute(x, "dp", [(d, d ^ k) for d in range(n_dp)])


def project_in(kept, blocks, me):
    rows = blocks[0].shape[0]
    total = None
    for k, b in enumerate(blocks):
        a = lax.dynamic_slice_in_dim(kept, (me ^ k) * rows, rows, axis=1)
        t = jnp.dot(a, b, preferred_element_type=F32)
        total = t if total is None else total + t
    return total.astype(BF16)


def mask_acts(acts, lengths):
    keep = (jnp.arange(acts.shape[1], dtype=jnp.int32)[None, :] < lengths[:, None]).astype(acts.dtype)
    return (acts * keep[:, :, None])[0]


def general(n_dp, acts, out_grads, basis_in, basis_out, lengths):
    seq = acts.shape[1]
    me = lax.axis_index("dp")
    kept = mask_acts(acts, lengths)

    def exchange(x, width):
        parts = [lax.dynamic_slice_in_dim(x, (me ^ k) * width, width, axis=1) for k in range(n_dp)]
        return [parts[0]] + [swap_dp(parts[k], k, n_dp) for k in range(1, n_dp)]

    far = swap_dp(basis_in, 2, n_dp)
    blocks = [basis_in, swap_dp(basis_in, 1, n_dp), far, swap_dp(far, 1, n_dp)]
    in_local = project_in(kept, blocks, me)
    n_chunks = 3
    step = seq // n_chunks
    outs = []
    for j in range(n_chunks):
        g = out_grads[0, j * step : (j + 1) * step]
        whole = lax.all_gather(g, "tensor", axis=1, tiled=True)
        mine = jnp.concatenate(exchange(whole, whole.shape[1] // n_dp), axis=0)
        part = jnp.dot(mine, basis_out, preferred_element_type=F32)
        part = part.reshape(n_dp, step, -1)
        odd = swap_dp(part[1::2].astype(BF16), 1, n_dp)
        s0 = part[0] + odd[0].astype(F32)
        s2 = part[2] + odd[1].astype(F32)
        far = swap_dp(jnp.stack([s2, s0]).astype(BF16), 2, n_dp)
        even = jnp.stack([s0 + far[0].astype(F32), s2 + far[1].astype(F32)]).astype(BF16)
        rest = swap_dp(even, 1, n_dp)
        outs.append(jnp.stack([even[0], rest[0], even[1], rest[1]]))
    in_all = lax.all_gather(in_local, "tensor", axis=1, tiled=True)
    in_proj = jnp.stack(exchange(in_all, in_all.shape[1] // n_dp))
    out_proj = jnp.concatenate(outs, axis=1).reshape(n_dp * seq, -1)
    return squares(jnp.arange(n_dp, dtype=jnp.int32) * seq, out_proj, in_proj)


def home_pairs(hops, across=False):
    pairs = []
    for x in (0, 1):
        for c in (0, 1):
            d = 2 * x + c
            for w0, w1 in hops:
                z0, z1 = (w0, w1) if x == 0 else (3 - w0, 3 - w1)
                if across:
                    pairs.append((z0 * 4 + (d ^ 2), z1 * 4 + d))
                else:
                    pairs.append((z0 * 4 + d, z1 * 4 + d))
    return pairs


def send(x, hops, across=False):
    return lax.ppermute(x, ("tensor", "dp"), home_pairs(hops, across))


def to_home(x):
    return send(x, [(0, 0), (1, 1)], True)


def tie(v, *after):
    return lax.optimization_barrier((v,) + after)[0]


def swap(v, k=1):
    return swap_dp(v, k, 4)


def compact(cap, acts, grads, basis_in, basis_out, lens):
    seq = acts.shape[1]
    me = lax.axis_index("dp")
    z = lax.axis_index("tensor")
    x, c = me // 2, me % 2
    w = jnp.where(x == 0, z, 3 - z)
    m = STEPS
    u = cap // m
    c2 = min(m, -(-min(2 * seq, cap - 2 * MIN_LEN) // u))
    want_outer = c == x
    kept = mask_acts(acts, lax.dynamic_slice_in_dim(lens, me, 1))

    al = (lens + ALIGN - 1) // ALIGN * ALIGN
    off = jnp.stack([jnp.int32(0), al[0], cap - al[3] - al[2], cap - al[3]])

    pos = jnp.arange(c2 * u, dtype=jnp.int32)
    chunk = pos // u
    row = jnp.where(x == 0, chunk, m - 1 - chunk) * u + pos % u
    s = jnp.arange(seq, dtype=jnp.int32)

    def pick(n):
        return (row[:, None] == (off[n] + s)[None, :]) & (s < lens[n])[None, :]

    hot = jnp.concatenate([pick(me), pick(me ^ 1)], axis=1).astype(BF16)

    def pack(v):
        return jnp.dot(hot, v, preferred_element_type=F32).astype(BF16).reshape(c2, u, v.shape[1])

    def merged(own, others, i):
        t = None
        if i < c2:
            t = own[i]
        if m - 1 - i < c2:
            o = others[m - 1 - i]
            t = o if t is None else t + o
        return t

    def halves(outer, inner):
        mine = jnp.where(want_outer, outer, inner)
        return mine, swap(jnp.where(want_outer, inner, outer))

    packed = pack(grads)
    arrived = [None] * c2
    last = None
    for i in range(c2 - 1, -1, -1):
        arrived[i] = to_home(packed[i] if last is None else tie(packed[i], last))
        last = arrived[i]
    far_in = swap(tie(basis_in, last), 2)
    near_in = swap(tie(basis_in, arrived[c2 - 1]))
    far_near = swap(far_in)

    blocks, given, held, sums, fars = ([None] * m for _ in range(5))
    own, fa, fb, m1 = [None] * m, [None] * (m + 1), [None] * m, [None] * m

    def meet(i):
        outer = jnp.where(w == 0, own[i], jnp.where(w == 1, fa[i], jnp.where(w == 2, fb[i], fa[i + 1])))
        inner = jnp.where(w == 0, m1[i], jnp.where(w == 1, own[i], jnp.where(w == 2, fa[i], fb[i])))
        blocks[i] = halves(outer, inner)

    def product(i):
        given[i], held[i] = products(c, *blocks[i], basis_out)

    def add_core(i):
        sums[i] = held[i] + swap(given[i]).astype(F32)
        fars[i] = swap(sums[i].astype(BF16), 2)

    in_local = None
    for i in range(m):
        own[i] = merged(packed, arrived, i)
        v = own[i] if i == 0 else jnp.where(w == 2, fb[i - 1], own[i])
        fa[i] = send(tie(v, *([held[i - 3]] if i >= 3 else [])), [(0, 1), (1, 2)] + ([(2, 3)] if i else []))
        m1[i] = send(own[i], [(1, 0)])
        if i >= 1:
            meet(i - 1)
        if i >= 3:
            add_core(i - 3)
        after = []
        if i >= 2:
            after += blocks[i - 2]
            product(i - 2)
        if i >= 3:
            after.append(sums[i - 3])
        if i == m - 1:
            in_local = project_in(kept, [basis_in, near_in, far_in, far_near], me)
            after.append(in_local)
        fb[i] = send(tie(fa[i], *after), [(1, 2), (2, 3)])

    hc = in_local.shape[1] // 2
    in_mine = lax.dynamic_slice_in_dim(in_local, c * hc, hc, axis=1)
    in_given = lax.dynamic_slice_in_dim(in_local, (1 - c) * hc, hc, axis=1)
    in_packed = pack(jnp.concatenate([in_mine, swap(in_given)], axis=0))
    in_arrived = to_home(in_packed)
    in_own = jnp.concatenate([merged(in_packed, in_arrived, i) for i in range(m)], axis=0)

    after = [fb[m - 1], held[m - 3], fars[m - 4], blocks[m - 2][1]]
    fa[m] = send(tie(fb[m - 1], *after), [(2, 3)])
    r1 = send(tie(in_own, *after), [(0, 1), (1, 2)])
    i1 = send(in_own, [(1, 0)])
    add_core(m - 3)
    blocks[m - 2] = (tie(blocks[m - 2][0], fb[m - 1]), blocks[m - 2][1])
    product(m - 2)
    meet(m - 1)
    r2 = send(tie(r1, fa[m], fars[m - 3], held[m - 2]), [(1, 2), (2, 3)])
    add_core(m - 2)
    product(m - 1)
    r3 = send(tie(r2, sums[m - 2], held[m - 1]), [(2, 3)])
    add_core(m - 1)
    outer = jnp.where(w == 0, in_own, jnp.where(w == 1, r1, jnp.where(w == 2, r2, r3)))
    inner = jnp.where(w == 0, i1, jnp.where(w == 1, in_own, jnp.where(w == 2, r1, r2)))
    mine, other = halves(outer, inner)
    in_t = jnp.where(c == 0, jnp.concatenate([mine, other], 1), jnp.concatenate([other, mine], 1))
    in_t = in_t.reshape(m, u, 2 * hc)
    in_t = jnp.where(x == 0, in_t, in_t[::-1]).reshape(cap, 2 * hc)

    mine, rest = [None] * (m // 2), [None] * (m // 2)
    for j in range(m // 2 - 1, -1, -1):
        k = m - 1 - j
        lo = jnp.where(x == 0, sums[j], sums[k]) + jnp.where(x == 0, fars[k], fars[j]).astype(F32)
        hi = jnp.where(x == 0, sums[k], sums[j]) + jnp.where(x == 0, fars[j], fars[k]).astype(F32)
        mine[j] = jnp.stack([lo, hi]).astype(BF16)
        rest[j] = swap(mine[j])

    ends = off + al
    starts = jnp.stack([off[0], off[1], ends[2] - seq, ends[3] - seq]).astype(jnp.int32)
    wins = []
    for n in range(4):
        rows = starts[n] + s
        valid = (rows >= off[n]) & (rows < off[n] + lens[n])
        win = lax.dynamic_slice_in_dim(in_t, starts[n], seq, axis=0)
        wins.append(jnp.where(valid[:, None], win, jnp.zeros_like(win)))
    return squares_of_pieces(starts, c, mine, rest, jnp.stack(wins))


def special(caps, acts, out_grads, basis_in, basis_out, lengths):
    me = lax.axis_index("dp")
    c = me % 2
    every = lax.all_gather(lengths, ("groups", "dp"), axis=0, tiled=True)
    g = out_grads[0]
    half = g.shape[1] // 2
    mine = lax.dynamic_slice_in_dim(g, c * half, half, axis=1)
    given = lax.dynamic_slice_in_dim(g, (1 - c) * half, half, axis=1)
    grads = jnp.concatenate([mine, swap_dp(given, 1, 4)], axis=0)
    totals = jnp.sum(((every + ALIGN - 1) // ALIGN * ALIGN).reshape(-1, 4), axis=1)
    need = jnp.max(totals)
    lens = lax.dynamic_slice_in_dim(every, lax.axis_index("groups") * 4, 4)
    index = jnp.int32(0)
    for cap in caps[:-1]:
        index = index + (need > cap).astype(jnp.int32)
    branches = [functools.partial(compact, cap) for cap in caps]
    return lax.switch(index, branches, acts, grads, basis_in, basis_out, lens)


def per_device(sizes, caps, acts, out_grads, basis_in, basis_out, lengths):
    if sizes == (4, 4):
        return special(caps, acts, out_grads, basis_in, basis_out, lengths)
    return general(sizes[1], acts, out_grads, basis_in, basis_out, lengths)


CAPS = (768, 832, 896, 960, 1152)


def solution(mesh):
    in_specs = (
        P(("groups", "dp"), None, None),
        P(("groups", "dp"), None, "tensor"),
        P(("groups", "dp"), "tensor"),
        P(("groups", "dp"), "tensor"),
        P(("groups", "dp")),
    )
    out_specs = P(("groups", "tensor"), "dp")
    sizes = (mesh.shape["tensor"], mesh.shape["dp"])
    return jax.shard_map(
        functools.partial(per_device, sizes, CAPS), mesh=mesh, in_specs=in_specs, out_specs=out_specs, check_vma=False
    )
```

profile of v0, /device:TPU:3, one launch (start us, length us, event | category | flops | bytes accessed | tf_op | source)
XLA Modules:
  0.0 345.5 jit_solution(1396969281412203105)
XLA Ops:
  4.4 5.4 %all-reduce = s32[8]{0:T(128)S(1)} all-reduce(s32[8]{0:T(128)S(1)} %dynamic-update-slice), channel_id=1, replica_groups=mesh['groups'=2,'tensor'=4,'dp'=4] {'groups','dp'}, use_global_device_ids=true, to_apply=%add | all-reduce | flops 8 | bytes 64
  14.7 329.8 %conditional.1 = (bf16[3584,1024]{1,0:T(8,128)(2,1)}) conditional(s32[]{:T(128)} %clamp.3, (s32[8]{0:T(128)S(1)}, bf16[576,1792]{1,0:T(8,128)(2,1)}, bf16[3584,3584]{1,0:T(8,128)(2,1)}, bf16[1,288,4096]{2,1,0:T(8,128)(2,1)}, bf16[1024,1024]{1,0:T(8,128)(2,1)}, /*index=5*/s32[]{:T(128)}, s32[]{:T(128)}, (), s32[]{:T(128)}, ...), branch_computations={%region_2.3_spmd, %region_3.4_spmd, %region_4.5_spmd, %region_5.6_... | conditional | flops 4393529856 | bytes 410726432 | solution.py:379
  30.1 3.7 %convolution_convert_fusion.4 = bf16[672,1792]{1,0:T(8,128)(2,1)S(1)} fusion(bf16[576,1792]{1,0:T(8,128)(2,1)} %get-tuple-element.112, pred[672,288]{1,0:T(32,128)(4,1)S(1)} %get-tuple-element.509, pred[672,288]{1,0:T(32,128)(4,1)S(1)} %get-tuple-element.508), kind=kOutput, calls=%fused_computation.252 | convolution fusion | flops 1388857344 | bytes 4859904 | tf_op jit(solution)/shard_map/cond/branch_2_fun/dot_general | solution.py:256
  35.8 6.6 %collective-permute-start.82 = (bf16[224,1792]{1,0:T(8,128)(2,1)}, bf16[224,1792]{1,0:T(8,128)(2,1)}, u32[]{:S(2)}, u32[]{:S(2)}) collective-permute-start(bf16[224,1792]{1,0:T(8,128)(2,1)} %get-tuple-element.494), channel_id=1, source_target_pairs={{2,0},{6,4},{3,1},{7,5},{12,14},{8,10},{13,15},{9,11},{18,16},{22,... | collective-permute-start | bytes 2408456 | tf_op jit(solution)/shard_map/cond/branch_2_fun/ppermute | solution.py:215
  43.7 13.2 %collective-permute-done.82 = bf16[224,1792]{1,0:T(8,128)(2,1)} collective-permute-done((bf16[224,1792]{1,0:T(8,128)(2,1)}, bf16[224,1792]{1,0:T(8,128)(2,1)}, u32[]{:S(2)}, u32[]{:S(2)}) %collective-permute-start.82) | collective-permute-done | bytes 802848 | tf_op jit(solution)/shard_map/cond/branch_2_fun/ppermute | solution.py:215
  56.9 16.2 %collective-permute-done.81 = bf16[224,1792]{1,0:T(8,128)(2,1)} collective-permute-done((bf16[224,1792]{1,0:T(8,128)(2,1)S(1)}, bf16[224,1792]{1,0:T(8,128)(2,1)}, u32[]{:S(2)}, u32[]{:S(2)}) %collective-permute-start.81) | collective-permute-done | bytes 802848 | tf_op jit(solution)/shard_map/cond/branch_2_fun/ppermute | solution.py:215
  76.6 6.3 %collective-permute-start.87 = (bf16[224,1792]{1,0:T(8,128)(2,1)}, bf16[224,1792]{1,0:T(8,128)(2,1)}, u32[]{:S(2)}, u32[]{:S(2)}) collective-permute-start(bf16[224,1792]{1,0:T(8,128)(2,1)} %get-tuple-element.116), channel_id=1, source_target_pairs={{2,0},{6,4},{3,1},{7,5},{12,14},{8,10},{13,15},{9,11},{18,16},{22,... | collective-permute-start | bytes 2408456 | tf_op jit(solution)/shard_map/cond/branch_2_fun/ppermute | solution.py:215
  84.4 8.6 %collective-permute-done.83 = bf16[224,1792]{1,0:T(8,128)(2,1)} collective-permute-done((bf16[224,1792]{1,0:T(8,128)(2,1)S(1)}, bf16[224,1792]{1,0:T(8,128)(2,1)}, u32[]{:S(2)}, u32[]{:S(2)}) %collective-permute-start.83) | collective-permute-done | bytes 802848 | tf_op jit(solution)/shard_map/cond/branch_2_fun/ppermute | solution.py:215
  95.5 4.1 %collective-permute-start.88 = (bf16[224,1792]{1,0:T(8,128)(2,1)}, bf16[224,1792]{1,0:T(8,128)(2,1)S(1)}, u32[]{:S(2)}, u32[]{:S(2)}) collective-permute-start(bf16[224,1792]{1,0:T(8,128)(2,1)} %get-tuple-element.117), channel_id=1, source_target_pairs={{2,0},{6,4},{3,1},{7,5},{12,14},{8,10},{13,15},{9,11},{18,16},{22,... | collective-permute-start | bytes 2408456 | tf_op jit(solution)/shard_map/cond/branch_2_fun/ppermute | solution.py:215
  99.7 10.4 %collective-permute-done.89 = bf16[224,1792]{1,0:T(8,128)(2,1)} collective-permute-done((bf16[224,1792]{1,0:T(8,128)(2,1)}, bf16[224,1792]{1,0:T(8,128)(2,1)}, u32[]{:S(2)}, u32[]{:S(2)}) %collective-permute-start.89) | collective-permute-done | bytes 802848 | tf_op jit(solution)/shard_map/cond/branch_2_fun/ppermute | solution.py:215
  110.1 3.1 broadcast_select_fusion.29
  114.7 5.5 %collective-permute-start.85 = (bf16[224,1792]{1,0:T(8,128)(2,1)S(1)}, bf16[224,1792]{1,0:T(8,128)(2,1)S(1)}, u32[]{:S(2)}, u32[]{:S(2)}) collective-permute-start(bf16[224,1792]{1,0:T(8,128)(2,1)S(1)} %get-tuple-element.490), channel_id=1, source_target_pairs={{0,1},{1,0},{2,3},{3,2},{4,5},{5,4},{6,7},{7,6},{8,9},{9,8},{10,11... | collective-permute-start | bytes 2408456 | tf_op jit(solution)/shard_map/cond/branch_2_fun/ppermute | solution.py:148
  120.8 4.0 %collective-permute-start.96 = (bf16[1024,1024]{1,0:T(8,128)(2,1)}, bf16[1024,1024]{1,0:T(8,128)(2,1)}, u32[]{:S(2)}, u32[]{:S(2)}) collective-permute-start(bf16[1024,1024]{1,0:T(8,128)(2,1)} %get-tuple-element.123), channel_id=1, source_target_pairs={{0,2},{1,3},{2,0},{3,1},{4,6},{5,7},{6,4},{7,5},{8,10},{9,11},{10,... | collective-permute-start | bytes 6291464 | tf_op jit(solution)/shard_map/cond/branch_2_fun/ppermute | solution.py:148
  124.9 4.4 %collective-permute-done.90 = bf16[224,1792]{1,0:T(8,128)(2,1)} collective-permute-done((bf16[224,1792]{1,0:T(8,128)(2,1)S(1)}, bf16[224,1792]{1,0:T(8,128)(2,1)}, u32[]{:S(2)}, u32[]{:S(2)}) %collective-permute-start.90) | collective-permute-done | bytes 802848 | tf_op jit(solution)/shard_map/cond/branch_2_fun/ppermute | solution.py:215
  132.2 2.6 fusion.112
  135.5 12.0 %branch_2_fun.5 = (bf16[224,1792]{1,0:T(8,128)(2,1)S(1)}, f32[224,1792]{1,0:T(8,128)S(1)}) custom-call(s32[1]{0:T(128)} %bitcast.75.c_ref, bf16[224,1792]{1,0:T(8,128)(2,1)S(1)} %broadcast_select_fusion.38.mine_ref, bf16[224,1792]{1,0:T(8,128)(2,1)S(1)} %collective-permute-done.85.other_ref, bf16[3584,3584]{1,0:T(8,128)(2,1)} %get-tuple-element.228.b_mine_ref.b_other_ref, ...), custom_call_target="tpu_custom_call" | custom-call | flops 1 | bytes 1 | tf_op jit(solution)/shard_map/cond/branch_2_fun/pallas_call | solution.py:74
  147.6 7.4 %collective-permute-start.86 = (bf16[224,1792]{1,0:T(8,128)(2,1)S(1)}, bf16[224,1792]{1,0:T(8,128)(2,1)S(1)}, u32[]{:S(2)}, u32[]{:S(2)}) collective-permute-start(bf16[224,1792]{1,0:T(8,128)(2,1)S(1)} %get-tuple-element.115), channel_id=1, source_target_pairs={{0,1},{1,0},{2,3},{3,2},{4,5},{5,4},{6,7},{7,6},{8,9},{9,8},{10,11... | collective-permute-start | bytes 2408456 | tf_op jit(solution)/shard_map/cond/branch_2_fun/ppermute | solution.py:148
  155.0 2.4 convolution_add_fusion.8
  159.6 11.1 %collective-permute-done.96 = bf16[1024,1024]{1,0:T(8,128)(2,1)} collective-permute-done((bf16[1024,1024]{1,0:T(8,128)(2,1)}, bf16[1024,1024]{1,0:T(8,128)(2,1)}, u32[]{:S(2)}, u32[]{:S(2)}) %collective-permute-start.96) | collective-permute-done | bytes 2097184 | tf_op jit(solution)/shard_map/cond/branch_2_fun/ppermute | solution.py:148
  173.4 2.4 convolution_add_fusion.7
  175.8 4.9 %collective-permute-done.92 = bf16[224,1792]{1,0:T(8,128)(2,1)S(1)} collective-permute-done((bf16[224,1792]{1,0:T(8,128)(2,1)S(1)}, bf16[224,1792]{1,0:T(8,128)(2,1)S(1)}, u32[]{:S(2)}, u32[]{:S(2)}) %collective-permute-start.92) | collective-permute-done | bytes 802848 | tf_op jit(solution)/shard_map/cond/branch_2_fun/ppermute | solution.py:215
  188.7 15.0 %collective-permute-start.114 = (bf16[3,224,512]{2,1,0:T(8,128)(2,1)S(1)}, bf16[3,224,512]{2,1,0:T(8,128)(2,1)S(1)}, u32[]{:S(2)}, u32[]{:S(2)}) collective-permute-start(bf16[3,224,512]{2,1,0:T(8,128)(2,1)S(1)} %bitcast.330), channel_id=1, source_target_pairs={{2,0},{6,4},{3,1},{7,5},{12,14},{8,10},{13,15},{9,11},{18,16},{22,... | collective-permute-start | bytes 2064392 | tf_op jit(solution)/shard_map/cond/branch_2_fun/ppermute | solution.py:215
  203.7 11.9 %branch_2_fun.6 = (bf16[224,1792]{1,0:T(8,128)(2,1)S(1)}, f32[224,1792]{1,0:T(8,128)S(1)}) custom-call(s32[1]{0:T(128)} %bitcast.75.c_ref, bf16[224,1792]{1,0:T(8,128)(2,1)S(1)} %broadcast_select_fusion.36.mine_ref, bf16[224,1792]{1,0:T(8,128)(2,1)S(1)} %collective-permute-done.94.other_ref, bf16[3584,3584]{1,0:T(8,128)(2,1)} %get-tuple-element.228.b_mine_ref.b_other_ref, ...), custom_call_target="tpu_custom_call" | custom-call | flops 1 | bytes 1 | tf_op jit(solution)/shard_map/cond/branch_2_fun/pallas_call | solution.py:74
  219.5 4.2 %collective-permute-start.110 = (bf16[224,1792]{1,0:T(8,128)(2,1)S(1)}, bf16[224,1792]{1,0:T(8,128)(2,1)S(1)}, u32[]{:S(2)}, u32[]{:S(2)}) collective-permute-start(bf16[224,1792]{1,0:T(8,128)(2,1)S(1)} %fusion.104), channel_id=1, source_target_pairs={{0,2},{1,3},{2,0},{3,1},{4,6},{5,7},{6,4},{7,5},{8,10},{9,11},{10,... | collective-permute-start | bytes 2408456 | tf_op jit(solution)/shard_map/cond/branch_2_fun/ppermute | solution.py:148
  223.7 11.8 %branch_2_fun.8 = (bf16[224,1792]{1,0:T(8,128)(2,1)S(1)}, f32[224,1792]{1,0:T(8,128)S(1)}) custom-call(s32[1]{0:T(128)} %bitcast.75.c_ref, bf16[224,1792]{1,0:T(8,128)(2,1)S(1)} %get-tuple-element.130.mine_ref, bf16[224,1792]{1,0:T(8,128)(2,1)S(1)} %collective-permute-done.101.other_ref, bf16[3584,3584]{1,0:T(8,128)(2,1)} %get-tuple-element.228.b_mine_ref.b_other_ref, ...), custom_call_target="tpu_custom_call" | custom-call | flops 1 | bytes 1 | tf_op jit(solution)/shard_map/cond/branch_2_fun/pallas_call | solution.py:74
  236.2 4.2 %collective-permute-done.102 = bf16[224,1792]{1,0:T(8,128)(2,1)S(1)} collective-permute-done((bf16[224,1792]{1,0:T(8,128)(2,1)S(1)}, bf16[224,1792]{1,0:T(8,128)(2,1)S(1)}, u32[]{:S(2)}, u32[]{:S(2)}) %collective-permute-start.102) | collective-permute-done | bytes 802848 | tf_op jit(solution)/shard_map/cond/branch_2_fun/ppermute | solution.py:215
  244.2 11.9 %branch_2_fun.7 = (bf16[224,1792]{1,0:T(8,128)(2,1)S(1)}, f32[224,1792]{1,0:T(8,128)S(1)}) custom-call(s32[1]{0:T(128)} %bitcast.75.c_ref, bf16[224,1792]{1,0:T(8,128)(2,1)S(1)} %broadcast_select_fusion.33.mine_ref, bf16[224,1792]{1,0:T(8,128)(2,1)S(1)} %collective-permute-done.104.other_ref, bf16[3584,3584]{1,0:T(8,128)(2,1)} %get-tuple-element.228.b_mine_ref.b_other_ref, ...), custom_call_target="tpu_custom_call" | custom-call | flops 1 | bytes 1 | tf_op jit(solution)/shard_map/cond/branch_2_fun/pallas_call | solution.py:74
  258.0 10.0 %collective-permute-done.116 = bf16[896,512]{1,0:T(8,128)(2,1)S(1)} collective-permute-done((bf16[896,512]{1,0:T(8,128)(2,1)S(1)}, bf16[896,512]{1,0:T(8,128)(2,1)S(1)}, u32[]{:S(2)}, u32[]{:S(2)}) %collective-permute-start.116) | collective-permute-done | bytes 917536 | tf_op jit(solution)/shard_map/cond/branch_2_fun/ppermute | solution.py:215
  271.8 18.5 %collective-permute-done.117 = bf16[896,512]{1,0:T(8,128)(2,1)S(1)} collective-permute-done((bf16[896,512]{1,0:T(8,128)(2,1)S(1)}, bf16[896,512]{1,0:T(8,128)(2,1)S(1)}, u32[]{:S(2)}, u32[]{:S(2)}) %collective-permute-start.117) | collective-permute-done | bytes 917536 | tf_op jit(solution)/shard_map/cond/branch_2_fun/ppermute | solution.py:215
  293.2 2.3 collective-permute-start.119
  305.8 2.8 maximum_select_fusion.2
  310.2 22.3 %branch_2_fun.9 = bf16[3584,1024]{1,0:T(8,128)(2,1)} custom-call(s32[4]{0:T(128)S(1)} %pad_add_fusion.16.start_ref, s32[1]{0:T(128)} %bitcast.75.c_ref, bf16[2,224,1792]{2,1,0:T(8,128)(2,1)S(1)} %pad_maximum_fusion.9.refs_0_, bf16[2,224,1792]{2,1,0:T(8,128)(2,1)S(1)} %pad_maximum_fusion.10.refs_1_, bf16[2,224,1792]{2,1,0:T(8,128)(2,1)} %collective-permute-done.111.refs_2_, ...), custom_call_target="tpu_custom_call" | custom-call | flops 1 | bytes 1 | tf_op jit(solution)/shard_map/cond/branch_2_fun/pallas_call | solution.py:130
  (136 shorter events, 62.9 us)
Async XLA Ops:
  35.8 21.1 %collective-permute-start.82 = (bf16[224,1792]{1,0:T(8,128)(2,1)}, bf16[224,1792]{1,0:T(8,128)(2,1)}, u32[]{:S(2)}, u32[]{:S(2)}) collective-permute-start(bf16[224,1792]{1,0:T(8,128)(2,1)} %get-tuple-element.494), channel_id=1, source_target_pairs={{2,0},{6,4},{3,1},{7,5},{12,14},{8,10},{13,15},{9,11},{18,16},{22,... | collective-permute-start | bytes 2408456 | tf_op jit(solution)/shard_map/cond/branch_2_fun/ppermute | solution.py:215
  42.4 30.7 %collective-permute-start.81 = (bf16[224,1792]{1,0:T(8,128)(2,1)S(1)}, bf16[224,1792]{1,0:T(8,128)(2,1)}, u32[]{:S(2)}, u32[]{:S(2)}) collective-permute-start(bf16[224,1792]{1,0:T(8,128)(2,1)S(1)} %collective-permute-done.80), channel_id=1, source_target_pairs={{4,8},{8,12},{5,9},{9,13},{10,6},{6,2},{11,7},{7,3},{20,24},{24,28... | collective-permute-start | bytes 2408456 | tf_op jit(solution)/shard_map/cond/branch_2_fun/ppermute | solution.py:215
  75.3 17.8 %collective-permute-start.83 = (bf16[224,1792]{1,0:T(8,128)(2,1)S(1)}, bf16[224,1792]{1,0:T(8,128)(2,1)}, u32[]{:S(2)}, u32[]{:S(2)}) collective-permute-start(bf16[224,1792]{1,0:T(8,128)(2,1)S(1)} %get-tuple-element.346), channel_id=1, source_target_pairs={{0,4},{4,8},{8,12},{1,5},{5,9},{9,13},{14,10},{10,6},{6,2},{15,11}... | collective-permute-start | bytes 2408456 | tf_op jit(solution)/shard_map/cond/branch_2_fun/ppermute | solution.py:215
  76.6 18.9 %collective-permute-start.87 = (bf16[224,1792]{1,0:T(8,128)(2,1)}, bf16[224,1792]{1,0:T(8,128)(2,1)}, u32[]{:S(2)}, u32[]{:S(2)}) collective-permute-start(bf16[224,1792]{1,0:T(8,128)(2,1)} %get-tuple-element.116), channel_id=1, source_target_pairs={{2,0},{6,4},{3,1},{7,5},{12,14},{8,10},{13,15},{9,11},{18,16},{22,... | collective-permute-start | bytes 2408456 | tf_op jit(solution)/shard_map/cond/branch_2_fun/ppermute | solution.py:215
  82.9 16.8 %collective-permute-start.84 = (bf16[224,1792]{1,0:T(8,128)(2,1)}, bf16[224,1792]{1,0:T(8,128)(2,1)}, u32[]{:S(2)}, u32[]{:S(2)}) collective-permute-start(bf16[224,1792]{1,0:T(8,128)(2,1)} %get-tuple-element.117), channel_id=1, source_target_pairs={{4,0},{5,1},{10,14},{11,15},{20,16},{21,17},{26,30},{27,31}} | collective-permute-start | bytes 2408456 | tf_op jit(solution)/shard_map/cond/branch_2_fun/ppermute | solution.py:215
  93.1 17.1 %collective-permute-start.89 = (bf16[224,1792]{1,0:T(8,128)(2,1)}, bf16[224,1792]{1,0:T(8,128)(2,1)}, u32[]{:S(2)}, u32[]{:S(2)}) collective-permute-start(bf16[224,1792]{1,0:T(8,128)(2,1)} %collective-permute-done.83), channel_id=1, source_target_pairs={{4,8},{8,12},{5,9},{9,13},{10,6},{6,2},{11,7},{7,3},{20,24},{24,28... | collective-permute-start | bytes 2408456 | tf_op jit(solution)/shard_map/cond/branch_2_fun/ppermute | solution.py:215
  95.5 25.3 %collective-permute-start.88 = (bf16[224,1792]{1,0:T(8,128)(2,1)}, bf16[224,1792]{1,0:T(8,128)(2,1)S(1)}, u32[]{:S(2)}, u32[]{:S(2)}) collective-permute-start(bf16[224,1792]{1,0:T(8,128)(2,1)} %get-tuple-element.117), channel_id=1, source_target_pairs={{2,0},{6,4},{3,1},{7,5},{12,14},{8,10},{13,15},{9,11},{18,16},{22,... | collective-permute-start | bytes 2408456 | tf_op jit(solution)/shard_map/cond/branch_2_fun/ppermute | solution.py:215
  113.2 16.1 %collective-permute-start.90 = (bf16[224,1792]{1,0:T(8,128)(2,1)S(1)}, bf16[224,1792]{1,0:T(8,128)(2,1)}, u32[]{:S(2)}, u32[]{:S(2)}) collective-permute-start(bf16[224,1792]{1,0:T(8,128)(2,1)S(1)} %get-tuple-element.339), channel_id=1, source_target_pairs={{0,4},{4,8},{8,12},{1,5},{5,9},{9,13},{14,10},{10,6},{6,2},{15,11}... | collective-permute-start | bytes 2408456 | tf_op jit(solution)/shard_map/cond/branch_2_fun/ppermute | solution.py:215
  114.7 14.6 %collective-permute-start.85 = (bf16[224,1792]{1,0:T(8,128)(2,1)S(1)}, bf16[224,1792]{1,0:T(8,128)(2,1)S(1)}, u32[]{:S(2)}, u32[]{:S(2)}) collective-permute-start(bf16[224,1792]{1,0:T(8,128)(2,1)S(1)} %get-tuple-element.490), channel_id=1, source_target_pairs={{0,1},{1,0},{2,3},{3,2},{4,5},{5,4},{6,7},{7,6},{8,9},{9,8},{10,11... | collective-permute-start | bytes 2408456 | tf_op jit(solution)/shard_map/cond/branch_2_fun/ppermute | solution.py:148
  120.2 34.9 %collective-permute-start.95 = (bf16[1024,1024]{1,0:T(8,128)(2,1)}, bf16[1024,1024]{1,0:T(8,128)(2,1)}, u32[]{:S(2)}, u32[]{:S(2)}) collective-permute-start(bf16[1024,1024]{1,0:T(8,128)(2,1)} %get-tuple-element.123), channel_id=1, source_target_pairs={{0,1},{1,0},{2,3},{3,2},{4,5},{5,4},{6,7},{7,6},{8,9},{9,8},{10,11... | collective-permute-start | bytes 6291464 | tf_op jit(solution)/shard_map/cond/branch_2_fun/ppermute | solution.py:148
  120.8 49.8 %collective-permute-start.96 = (bf16[1024,1024]{1,0:T(8,128)(2,1)}, bf16[1024,1024]{1,0:T(8,128)(2,1)}, u32[]{:S(2)}, u32[]{:S(2)}) collective-permute-start(bf16[1024,1024]{1,0:T(8,128)(2,1)} %get-tuple-element.123), channel_id=1, source_target_pairs={{0,2},{1,3},{2,0},{3,1},{4,6},{5,7},{6,4},{7,5},{8,10},{9,11},{10,... | collective-permute-start | bytes 6291464 | tf_op jit(solution)/shard_map/cond/branch_2_fun/ppermute | solution.py:148
  129.3 28.8 %collective-permute-start.91 = (bf16[224,1792]{1,0:T(8,128)(2,1)}, bf16[224,1792]{1,0:T(8,128)(2,1)S(1)}, u32[]{:S(2)}, u32[]{:S(2)}) collective-permute-start(bf16[224,1792]{1,0:T(8,128)(2,1)} %collective-permute-done.90), channel_id=1, source_target_pairs={{4,8},{8,12},{5,9},{9,13},{10,6},{6,2},{11,7},{7,3},{20,24},{24,28... | collective-permute-start | bytes 2408456 | tf_op jit(solution)/shard_map/cond/branch_2_fun/ppermute | solution.py:215
  134.8 41.0 %collective-permute-start.93 = (bf16[224,1792]{1,0:T(8,128)(2,1)S(1)}, bf16[224,1792]{1,0:T(8,128)(2,1)S(1)}, u32[]{:S(2)}, u32[]{:S(2)}) collective-permute-start(bf16[224,1792]{1,0:T(8,128)(2,1)S(1)} %get-tuple-element.347), channel_id=1, source_target_pairs={{4,0},{5,1},{10,14},{11,15},{20,16},{21,17},{26,30},{27,31}} | collective-permute-start | bytes 2408456 | tf_op jit(solution)/shard_map/cond/branch_2_fun/ppermute | solution.py:215
  147.6 24.1 %collective-permute-start.86 = (bf16[224,1792]{1,0:T(8,128)(2,1)S(1)}, bf16[224,1792]{1,0:T(8,128)(2,1)S(1)}, u32[]{:S(2)}, u32[]{:S(2)}) collective-permute-start(bf16[224,1792]{1,0:T(8,128)(2,1)S(1)} %get-tuple-element.115), channel_id=1, source_target_pairs={{0,1},{1,0},{2,3},{3,2},{4,5},{5,4},{6,7},{7,6},{8,9},{9,8},{10,11... | collective-permute-start | bytes 2408456 | tf_op jit(solution)/shard_map/cond/branch_2_fun/ppermute | solution.py:148
  157.4 18.4 %collective-permute-start.100 = (bf16[224,1792]{1,0:T(8,128)(2,1)S(1)}, bf16[224,1792]{1,0:T(8,128)(2,1)S(1)}, u32[]{:S(2)}, u32[]{:S(2)}) collective-permute-start(bf16[224,1792]{1,0:T(8,128)(2,1)S(1)} %copy-done.17), channel_id=1, source_target_pairs={{4,0},{5,1},{10,14},{11,15},{20,16},{21,17},{26,30},{27,31}} | collective-permute-start | bytes 2408456 | tf_op jit(solution)/shard_map/cond/branch_2_fun/ppermute | solution.py:215
  158.3 22.4 %collective-permute-start.92 = (bf16[224,1792]{1,0:T(8,128)(2,1)S(1)}, bf16[224,1792]{1,0:T(8,128)(2,1)S(1)}, u32[]{:S(2)}, u32[]{:S(2)}) collective-permute-start(bf16[224,1792]{1,0:T(8,128)(2,1)S(1)} %broadcast_select_fusion.28), channel_id=1, source_target_pairs={{0,4},{4,8},{8,12},{1,5},{5,9},{9,13},{14,10},{10,6},{6,2},{15,11}... | collective-permute-start | bytes 2408456 | tf_op jit(solution)/shard_map/cond/branch_2_fun/ppermute | solution.py:215
  171.9 44.5 %collective-permute-start.99 = (bf16[224,1792]{1,0:T(8,128)(2,1)S(1)}, bf16[224,1792]{1,0:T(8,128)(2,1)S(1)}, u32[]{:S(2)}, u32[]{:S(2)}) collective-permute-start(bf16[224,1792]{1,0:T(8,128)(2,1)S(1)} %get-tuple-element.341), channel_id=1, source_target_pairs={{0,2},{1,3},{2,0},{3,1},{4,6},{5,7},{6,4},{7,5},{8,10},{9,11},{10,... | collective-permute-start | bytes 2408456 | tf_op jit(solution)/shard_map/cond/branch_2_fun/ppermute | solution.py:148
  182.8 34.2 %collective-permute-start.101 = (bf16[224,1792]{1,0:T(8,128)(2,1)S(1)}, bf16[224,1792]{1,0:T(8,128)(2,1)S(1)}, u32[]{:S(2)}, u32[]{:S(2)}) collective-permute-start(bf16[224,1792]{1,0:T(8,128)(2,1)S(1)} %broadcast_select_fusion.34), channel_id=1, source_target_pairs={{0,1},{1,0},{2,3},{3,2},{4,5},{5,4},{6,7},{7,6},{8,9},{9,8},{10,11... | collective-permute-start | bytes 2408456 | tf_op jit(solution)/shard_map/cond/branch_2_fun/ppermute | solution.py:148
  186.7 30.4 %collective-permute-start.98 = (bf16[224,1792]{1,0:T(8,128)(2,1)S(1)}, bf16[224,1792]{1,0:T(8,128)(2,1)S(1)}, u32[]{:S(2)}, u32[]{:S(2)}) collective-permute-start(bf16[224,1792]{1,0:T(8,128)(2,1)S(1)} %collective-permute-done.92), channel_id=1, source_target_pairs={{4,8},{8,12},{5,9},{9,13},{10,6},{6,2},{11,7},{7,3},{20,24},{24,28... | collective-permute-start | bytes 2408456 | tf_op jit(solution)/shard_map/cond/branch_2_fun/ppermute | solution.py:215
  188.7 29.7 %collective-permute-start.114 = (bf16[3,224,512]{2,1,0:T(8,128)(2,1)S(1)}, bf16[3,224,512]{2,1,0:T(8,128)(2,1)S(1)}, u32[]{:S(2)}, u32[]{:S(2)}) collective-permute-start(bf16[3,224,512]{2,1,0:T(8,128)(2,1)S(1)} %bitcast.330), channel_id=1, source_target_pairs={{2,0},{6,4},{3,1},{7,5},{12,14},{8,10},{13,15},{9,11},{18,16},{22,... | collective-permute-start | bytes 2064392 | tf_op jit(solution)/shard_map/cond/branch_2_fun/ppermute | solution.py:215
  216.4 19.8 %collective-permute-start.103 = (bf16[224,1792]{1,0:T(8,128)(2,1)S(1)}, bf16[224,1792]{1,0:T(8,128)(2,1)S(1)}, u32[]{:S(2)}, u32[]{:S(2)}) collective-permute-start(bf16[224,1792]{1,0:T(8,128)(2,1)S(1)} %copy-done.19), channel_id=1, source_target_pairs={{4,0},{5,1},{10,14},{11,15},{20,16},{21,17},{26,30},{27,31}} | collective-permute-start | bytes 2408456 | tf_op jit(solution)/shard_map/cond/branch_2_fun/ppermute | solution.py:215
  217.1 23.3 %collective-permute-start.102 = (bf16[224,1792]{1,0:T(8,128)(2,1)S(1)}, bf16[224,1792]{1,0:T(8,128)(2,1)S(1)}, u32[]{:S(2)}, u32[]{:S(2)}) collective-permute-start(bf16[224,1792]{1,0:T(8,128)(2,1)S(1)} %collective-permute-done.98), channel_id=1, source_target_pairs={{8,12},{9,13},{6,2},{7,3},{24,28},{25,29},{22,18},{23,19}} | collective-permute-start | bytes 2408456 | tf_op jit(solution)/shard_map/cond/branch_2_fun/ppermute | solution.py:215
  218.6 23.1 %collective-permute-start.115 = (bf16[896,512]{1,0:T(8,128)(2,1)S(1)}, bf16[896,512]{1,0:T(8,128)(2,1)S(1)}, u32[]{:S(2)}, u32[]{:S(2)}) collective-permute-start(bf16[896,512]{1,0:T(8,128)(2,1)S(1)} %pad_maximum_fusion.11), channel_id=1, source_target_pairs={{0,4},{4,8},{1,5},{5,9},{14,10},{10,6},{15,11},{11,7},{16,20},{20,... | collective-permute-start | bytes 2752520 | tf_op jit(solution)/shard_map/cond/branch_2_fun/ppermute | solution.py:215
  219.5 22.2 %collective-permute-start.110 = (bf16[224,1792]{1,0:T(8,128)(2,1)S(1)}, bf16[224,1792]{1,0:T(8,128)(2,1)S(1)}, u32[]{:S(2)}, u32[]{:S(2)}) collective-permute-start(bf16[224,1792]{1,0:T(8,128)(2,1)S(1)} %fusion.104), channel_id=1, source_target_pairs={{0,2},{1,3},{2,0},{3,1},{4,6},{5,7},{6,4},{7,5},{8,10},{9,11},{10,... | collective-permute-start | bytes 2408456 | tf_op jit(solution)/shard_map/cond/branch_2_fun/ppermute | solution.py:148
  241.7 26.3 %collective-permute-start.116 = (bf16[896,512]{1,0:T(8,128)(2,1)S(1)}, bf16[896,512]{1,0:T(8,128)(2,1)S(1)}, u32[]{:S(2)}, u32[]{:S(2)}) collective-permute-start(bf16[896,512]{1,0:T(8,128)(2,1)S(1)} %collective-permute-done.115), channel_id=1, source_target_pairs={{4,8},{8,12},{5,9},{9,13},{10,6},{6,2},{11,7},{7,3},{20,24},{24,28... | collective-permute-start | bytes 2752520 | tf_op jit(solution)/shard_map/cond/branch_2_fun/ppermute | solution.py:215
  243.2 26.1 %collective-permute-start.109 = (bf16[224,1792]{1,0:T(8,128)(2,1)S(1)}, bf16[224,1792]{1,0:T(8,128)(2,1)S(1)}, u32[]{:S(2)}, u32[]{:S(2)}) collective-permute-start(bf16[224,1792]{1,0:T(8,128)(2,1)S(1)} %get-tuple-element.328), channel_id=1, source_target_pairs={{0,2},{1,3},{2,0},{3,1},{4,6},{5,7},{6,4},{7,5},{8,10},{9,11},{10,... | collective-permute-start | bytes 2408456 | tf_op jit(solution)/shard_map/cond/branch_2_fun/ppermute | solution.py:148
  256.0 13.9 %collective-permute-start.105 = (bf16[224,1792]{1,0:T(8,128)(2,1)S(1)}, bf16[224,1792]{1,0:T(8,128)(2,1)S(1)}, u32[]{:S(2)}, u32[]{:S(2)}) collective-permute-start(bf16[224,1792]{1,0:T(8,128)(2,1)S(1)} %get-tuple-element.128), channel_id=1, source_target_pairs={{0,1},{1,0},{2,3},{3,2},{4,5},{5,4},{6,7},{7,6},{8,9},{9,8},{10,11... | collective-permute-start | bytes 2408456 | tf_op jit(solution)/shard_map/cond/branch_2_fun/ppermute | solution.py:148
  257.3 14.5 %collective-permute-start.118 = (bf16[896,512]{1,0:T(8,128)(2,1)S(1)}, bf16[896,512]{1,0:T(8,128)(2,1)S(1)}, u32[]{:S(2)}, u32[]{:S(2)}) collective-permute-start(bf16[896,512]{1,0:T(8,128)(2,1)S(1)} %pad_maximum_fusion.11), channel_id=1, source_target_pairs={{4,0},{5,1},{10,14},{11,15},{20,16},{21,17},{26,30},{27,31}} | collective-permute-start | bytes 2752520 | tf_op jit(solution)/shard_map/cond/branch_2_fun/ppermute | solution.py:215
  268.0 22.3 %collective-permute-start.117 = (bf16[896,512]{1,0:T(8,128)(2,1)S(1)}, bf16[896,512]{1,0:T(8,128)(2,1)S(1)}, u32[]{:S(2)}, u32[]{:S(2)}) collective-permute-start(bf16[896,512]{1,0:T(8,128)(2,1)S(1)} %collective-permute-done.116), channel_id=1, source_target_pairs={{8,12},{9,13},{6,2},{7,3},{24,28},{25,29},{22,18},{23,19}} | collective-permute-start | bytes 2752520 | tf_op jit(solution)/shard_map/cond/branch_2_fun/ppermute | solution.py:215
  270.1 25.4 %collective-permute-start.106 = (bf16[224,1792]{1,0:T(8,128)(2,1)S(1)}, bf16[224,1792]{1,0:T(8,128)(2,1)S(1)}, u32[]{:S(2)}, u32[]{:S(2)}) collective-permute-start(bf16[224,1792]{1,0:T(8,128)(2,1)S(1)} %fusion.103), channel_id=1, source_target_pairs={{0,2},{1,3},{2,0},{3,1},{4,6},{5,7},{6,4},{7,5},{8,10},{9,11},{10,... | collective-permute-start | bytes 2408456 | tf_op jit(solution)/shard_map/cond/branch_2_fun/ppermute | solution.py:148
  270.3 39.9 %collective-permute-start.112 = (bf16[2,224,1792]{2,1,0:T(8,128)(2,1)S(1)}, bf16[2,224,1792]{2,1,0:T(8,128)(2,1)}, u32[]{:S(2)}, u32[]{:S(2)}) collective-permute-start(bf16[2,224,1792]{2,1,0:T(8,128)(2,1)S(1)} %pad_maximum_fusion.10.refs_1_), channel_id=1, source_target_pairs={{0,1},{1,0},{2,3},{3,2},{4,5},{5,4},{6,7},{7,6},{8,9},{9,8},{10,11... | collective-permute-start | bytes 4816904 | tf_op jit(solution)/shard_map/cond/branch_2_fun/ppermute | solution.py:148
  296.3 13.9 %collective-permute-start.111 = (bf16[2,224,1792]{2,1,0:T(8,128)(2,1)S(1)}, bf16[2,224,1792]{2,1,0:T(8,128)(2,1)}, u32[]{:S(2)}, u32[]{:S(2)}) collective-permute-start(bf16[2,224,1792]{2,1,0:T(8,128)(2,1)S(1)} %pad_maximum_fusion.9.refs_0_), channel_id=1, source_target_pairs={{0,1},{1,0},{2,3},{3,2},{4,5},{5,4},{6,7},{7,6},{8,9},{9,8},{10,11... | collective-permute-start | bytes 4816904 | tf_op jit(solution)/shard_map/cond/branch_2_fun/ppermute | solution.py:148
  (18 other events, 156.3 us)
where the time goes:
time: 341 us; the launch traced here: 346 us
  waiting for transfers between devices  105 us (31%)
  starting transfers between devices  84.8 us (25%)
  Pallas kernels  70 us (21%)
  loops' own time  29.2 us (9%)
  other arithmetic  27.8 us (8%)
  matrix products  12.5 us (4%)
  local copies, waits for them, and re-layouts  6.97 us (2%)
  blocking collectives  5.36 us (2%)
  between operations  4.34 us (1%)
    ppermute x21, waiting for transfers between devices, send(): return lax.ppermute(x, ('tensor', 'dp'), home_pairs(hops, across))  91.6 us
    ppermute x21, starting transfers between devices, send(): return lax.ppermute(x, ('tensor', 'dp'), home_pairs(hops, across))  50.8 us
    pallas_call x4, Pallas kernels, products(): pl.pallas_call(product_kernel, grid_spec=pltpu.PrefetchScalarGridSpec(num...  47.6 us
    ppermute x20, starting transfers between devices, swap_dp(): return lax.ppermute(x, 'dp', [(d, d ^ k) for d in range(n_dp)])  34 us
    another operation x1, loops' own time, special(): return lax.switch(index, branches, acts, grads, basis_in, basis_out, lens)  29.2 us
    pallas_call x1, Pallas kernels, squares_of_pieces(): pl.pallas_call(functools.partial(pieces_kernel, pairs), grid_spec=pltpu.P...  22.3 us
    ppermute x20, waiting for transfers between devices, swap_dp(): return lax.ppermute(x, 'dp', [(d, d ^ k) for d in range(n_dp)])  13 us
    dot_general x4, matrix products, project_in(): t = jnp.dot(a, b, preferred_element_type=F32)  8.1 us
  transfers between devices with their start and end apart: 41, of which 13 were waited for; matrix products, arithmetic and copies ran while one was open for 9% of the time, Pallas kernels for 14%

commit v1 on v0

--- a/solution.py
+++ b/solution.py
@@ -124,7 +124,7 @@
     pairs = len(own)
     u, cols = own[0].shape[1:]
     n, seq, ins = wins.shape
-    tile = TILE
+    tile = 896 if cols % 896 == 0 else TILE
     per = cols // tile
     at = lambda i, s, c: (jnp.where(i < per, c[0] * per + i, (1 - c[0]) * per + i - per), 0)
     return pl.pallas_call(

time: 341 us -> 326 us (0.956); the launches traced: 346 us -> 322 us
  waiting for transfers between devices: 105 us -> 71.5 us
  other arithmetic: 27.8 us -> 37.5 us
  Pallas kernels: 70 us -> 64.5 us
    ppermute x21, waiting for transfers between devices: 91.6 us -> 66.5 us  [send(): return lax.ppermute(x, ('tensor', 'dp'), home_pairs(hops, across))]
    ppermute x20, waiting for transfers between devices: 13 us -> 5.06 us  [swap_dp(): return lax.ppermute(x, 'dp', [(d, d ^ k) for d in range(n_dp)])]
    ppermute x21, starting transfers between devices: 50.8 us -> 43.4 us  [send(): return lax.ppermute(x, ('tensor', 'dp'), home_pairs(hops, across))]
    ppermute x20, starting transfers between devices: 34 us -> 41 us  [swap_dp(): return lax.ppermute(x, 'dp', [(d, d ^ k) for d in range(n_dp)])]
    convert_element_type x4, other arithmetic: 0.65 us -> 4.68 us  [add_core(): fars[i] = swap(sums[i].astype(BF16), 2)]
  transfers between devices with their start and end apart: 41 -> 41, of which waited for: 13 -> 11; matrix products, arithmetic and copies ran while one was open for 9% -> 14% of each run, Pallas kernels for 14% -> 14%
where the time goes in v1:
time: 326 us; the launch traced here: 322 us
  starting transfers between devices  84.4 us (26%)
  waiting for transfers between devices  71.5 us (22%)
  Pallas kernels  64.5 us (20%)
  other arithmetic  37.5 us (12%)
  loops' own time  29.5 us (9%)
  matrix products  15.1 us (5%)
  local copies, waits for them, and re-layouts  9.38 us (3%)
  blocking collectives  5.36 us (2%)
  between operations  4.34 us (1%)
    ppermute x21, waiting for transfers between devices, send(): return lax.ppermute(x, ('tensor', 'dp'), home_pairs(hops, across))  66.5 us
    pallas_call x4, Pallas kernels, products(): pl.pallas_call(product_kernel, grid_spec=pltpu.PrefetchScalarGridSpec(num...  45.4 us
    ppermute x21, starting transfers between devices, send(): return lax.ppermute(x, ('tensor', 'dp'), home_pairs(hops, across))  43.4 us
    ppermute x20, starting transfers between devices, swap_dp(): return lax.ppermute(x, 'dp', [(d, d ^ k) for d in range(n_dp)])  41 us
    another operation x1, loops' own time, special(): return lax.switch(index, branches, acts, grads, basis_in, basis_out, lens)  29.5 us
    pallas_call x1, Pallas kernels, squares_of_pieces(): pl.pallas_call(functools.partial(pieces_kernel, pairs), grid_spec=pltpu.P...  19.1 us
    dot_general x4, matrix products, project_in(): t = jnp.dot(a, b, preferred_element_type=F32)  9.09 us
  transfers between devices with their start and end apart: 41, of which 11 were waited for; matrix products, arithmetic and copies ran while one was open for 14% of the time, Pallas kernels for 14%

profile of v1, /device:TPU:3, one launch (start us, length us, event | category | flops | bytes accessed | tf_op | source)
XLA Modules:
  0.0 321.6 jit_solution(11975177688993053046)
XLA Ops:
  4.4 5.4 %all-reduce = s32[8]{0:T(128)S(1)} all-reduce(s32[8]{0:T(128)S(1)} %dynamic-update-slice), channel_id=1, replica_groups=mesh['groups'=2,'tensor'=4,'dp'=4] {'groups','dp'}, use_global_device_ids=true, to_apply=%add | all-reduce | flops 8 | bytes 64
  14.7 305.9 %conditional.1 = (bf16[3584,1024]{1,0:T(8,128)(2,1)}) conditional(s32[]{:T(128)} %clamp.3, (s32[8]{0:T(128)S(1)}, bf16[576,1792]{1,0:T(8,128)(2,1)}, bf16[3584,3584]{1,0:T(8,128)(2,1)}, bf16[1,288,4096]{2,1,0:T(8,128)(2,1)}, bf16[1024,1024]{1,0:T(8,128)(2,1)}, /*index=5*/s32[]{:T(128)}, s32[]{:T(128)}, (), s32[]{:T(128)}, ...), branch_computations={%region_2.3_spmd, %region_3.4_spmd, %region_4.5_spmd, %region_5.6_... | conditional | flops 4393529856 | bytes 410726432 | solution.py:379
  21.4 3.5 %convolution_convert_fusion = bf16[576,1792]{1,0:T(8,128)(2,1)S(1)} fusion(bf16[576,1792]{1,0:T(8,128)(2,1)} %get-tuple-element.60, pred[576,288]{1,0:T(32,128)(4,1)S(1)} %get-tuple-element.425, pred[576,288]{1,0:T(32,128)(4,1)S(1)} %get-tuple-element.424), kind=kOutput, calls=%fused_computation | convolution fusion | flops 1190449152 | bytes 4460544 | tf_op jit(solution)/shard_map/cond/branch_0_fun/dot_general | solution.py:256
  27.5 6.5 %collective-permute-start.2 = (bf16[192,1792]{1,0:T(8,128)(2,1)S(1)}, bf16[192,1792]{1,0:T(8,128)(2,1)}, u32[]{:S(2)}, u32[]{:S(2)}) collective-permute-start(bf16[192,1792]{1,0:T(8,128)(2,1)S(1)} %get-tuple-element.410), channel_id=1, source_target_pairs={{2,0},{6,4},{3,1},{7,5},{12,14},{8,10},{13,15},{9,11},{18,16},{22,... | collective-permute-start | bytes 2064392 | tf_op jit(solution)/shard_map/cond/branch_0_fun/ppermute | solution.py:215
  35.3 10.5 %collective-permute-done.2 = bf16[192,1792]{1,0:T(8,128)(2,1)} collective-permute-done((bf16[192,1792]{1,0:T(8,128)(2,1)S(1)}, bf16[192,1792]{1,0:T(8,128)(2,1)}, u32[]{:S(2)}, u32[]{:S(2)}) %collective-permute-start.2) | collective-permute-done | bytes 688160 | tf_op jit(solution)/shard_map/cond/branch_0_fun/ppermute | solution.py:215
  45.8 13.4 %collective-permute-done.1 = bf16[192,1792]{1,0:T(8,128)(2,1)S(1)} collective-permute-done((bf16[192,1792]{1,0:T(8,128)(2,1)}, bf16[192,1792]{1,0:T(8,128)(2,1)S(1)}, u32[]{:S(2)}, u32[]{:S(2)}) %collective-permute-start.1) | collective-permute-done | bytes 688160 | tf_op jit(solution)/shard_map/cond/branch_0_fun/ppermute | solution.py:215
  59.2 2.7 broadcast_select_fusion.4
  63.1 5.5 %collective-permute-start.7 = (bf16[192,1792]{1,0:T(8,128)(2,1)}, bf16[192,1792]{1,0:T(8,128)(2,1)}, u32[]{:S(2)}, u32[]{:S(2)}) collective-permute-start(bf16[192,1792]{1,0:T(8,128)(2,1)} %get-tuple-element.66), channel_id=1, source_target_pairs={{2,0},{6,4},{3,1},{7,5},{12,14},{8,10},{13,15},{9,11},{18,16},{22,... | collective-permute-start | bytes 2064392 | tf_op jit(solution)/shard_map/cond/branch_0_fun/ppermute | solution.py:215
  70.2 6.9 %collective-permute-done.3 = bf16[192,1792]{1,0:T(8,128)(2,1)S(1)} collective-permute-done((bf16[192,1792]{1,0:T(8,128)(2,1)S(1)}, bf16[192,1792]{1,0:T(8,128)(2,1)S(1)}, u32[]{:S(2)}, u32[]{:S(2)}) %collective-permute-start.3) | collective-permute-done | bytes 688160 | tf_op jit(solution)/shard_map/cond/branch_0_fun/ppermute | solution.py:215
  79.0 4.1 %collective-permute-start.8 = (bf16[192,1792]{1,0:T(8,128)(2,1)}, bf16[192,1792]{1,0:T(8,128)(2,1)S(1)}, u32[]{:S(2)}, u32[]{:S(2)}) collective-permute-start(bf16[192,1792]{1,0:T(8,128)(2,1)} %get-tuple-element.67), channel_id=1, source_target_pairs={{2,0},{6,4},{3,1},{7,5},{12,14},{8,10},{13,15},{9,11},{18,16},{22,... | collective-permute-start | bytes 2064392 | tf_op jit(solution)/shard_map/cond/branch_0_fun/ppermute | solution.py:215
  83.1 8.3 %collective-permute-done.9 = bf16[192,1792]{1,0:T(8,128)(2,1)} collective-permute-done((bf16[192,1792]{1,0:T(8,128)(2,1)S(1)}, bf16[192,1792]{1,0:T(8,128)(2,1)}, u32[]{:S(2)}, u32[]{:S(2)}) %collective-permute-start.9) | collective-permute-done | bytes 688160 | tf_op jit(solution)/shard_map/cond/branch_0_fun/ppermute | solution.py:215
  91.5 2.8 broadcast_select_fusion.3
  95.6 5.5 %collective-permute-start.5 = (bf16[192,1792]{1,0:T(8,128)(2,1)S(1)}, bf16[192,1792]{1,0:T(8,128)(2,1)S(1)}, u32[]{:S(2)}, u32[]{:S(2)}) collective-permute-start(bf16[192,1792]{1,0:T(8,128)(2,1)S(1)} %get-tuple-element.406), channel_id=1, source_target_pairs={{0,1},{1,0},{2,3},{3,2},{4,5},{5,4},{6,7},{7,6},{8,9},{9,8},{10,11... | collective-permute-start | bytes 2064392 | tf_op jit(solution)/shard_map/cond/branch_0_fun/ppermute | solution.py:148
  101.8 2.9 collective-permute-start.16
  104.8 3.0 collective-permute-done.10
  110.7 2.6 fusion.12
  114.8 11.5 %branch_0_fun.5 = (bf16[192,1792]{1,0:T(8,128)(2,1)S(1)}, f32[192,1792]{1,0:T(8,128)S(1)}) custom-call(s32[1]{0:T(128)} %bitcast.3.c_ref, bf16[192,1792]{1,0:T(8,128)(2,1)S(1)} %broadcast_select_fusion.12.mine_ref, bf16[192,1792]{1,0:T(8,128)(2,1)S(1)} %collective-permute-done.5.other_ref, bf16[3584,3584]{1,0:T(8,128)(2,1)} %get-tuple-element.226.b_mine_ref.b_other_ref, ...), custom_call_target="tpu_custom_call" | custom-call | flops 1 | bytes 1 | tf_op jit(solution)/shard_map/cond/branch_0_fun/pallas_call | solution.py:74
  126.3 7.5 %collective-permute-start.6 = (bf16[192,1792]{1,0:T(8,128)(2,1)S(1)}, bf16[192,1792]{1,0:T(8,128)(2,1)S(1)}, u32[]{:S(2)}, u32[]{:S(2)}) collective-permute-start(bf16[192,1792]{1,0:T(8,128)(2,1)S(1)} %get-tuple-element.65), channel_id=1, source_target_pairs={{0,1},{1,0},{2,3},{3,2},{4,5},{5,4},{6,7},{7,6},{8,9},{9,8},{10,11... | collective-permute-start | bytes 2064392 | tf_op jit(solution)/shard_map/cond/branch_0_fun/ppermute | solution.py:148
  139.1 8.1 %collective-permute-start.19 = (bf16[192,1792]{1,0:T(8,128)(2,1)}, bf16[192,1792]{1,0:T(8,128)(2,1)}, u32[]{:S(2)}, u32[]{:S(2)}) collective-permute-start(bf16[192,1792]{1,0:T(8,128)(2,1)} %get-tuple-element.287), channel_id=1, source_target_pairs={{0,2},{1,3},{2,0},{3,1},{4,6},{5,7},{6,4},{7,5},{8,10},{9,11},{10,... | collective-permute-start | bytes 2064392 | tf_op jit(solution)/shard_map/cond/branch_0_fun/ppermute | solution.py:148
  147.3 3.5 %collective-permute-done.16 = bf16[1024,1024]{1,0:T(8,128)(2,1)} collective-permute-done((bf16[1024,1024]{1,0:T(8,128)(2,1)}, bf16[1024,1024]{1,0:T(8,128)(2,1)}, u32[]{:S(2)}, u32[]{:S(2)}) %collective-permute-start.16) | collective-permute-done | bytes 2097184 | tf_op jit(solution)/shard_map/cond/branch_0_fun/ppermute | solution.py:148
  157.5 2.4 convolution_add_fusion.1
  163.1 11.3 %branch_0_fun.6 = (bf16[192,1792]{1,0:T(8,128)(2,1)S(1)}, f32[192,1792]{1,0:T(8,128)S(1)}) custom-call(s32[1]{0:T(128)} %bitcast.3.c_ref, bf16[192,1792]{1,0:T(8,128)(2,1)S(1)} %broadcast_select_fusion.10.mine_ref, bf16[192,1792]{1,0:T(8,128)(2,1)S(1)} %collective-permute-done.14.other_ref, bf16[3584,3584]{1,0:T(8,128)(2,1)} %get-tuple-element.226.b_mine_ref.b_other_ref, ...), custom_call_target="tpu_custom_call" | custom-call | flops 1 | bytes 1 | tf_op jit(solution)/shard_map/cond/branch_0_fun/pallas_call | solution.py:74
  177.8 2.5 convolution_convert_fusion.1
  180.3 6.4 %collective-permute-start.34 = (bf16[3,192,512]{2,1,0:T(8,128)(2,1)}, bf16[3,192,512]{2,1,0:T(8,128)(2,1)}, u32[]{:S(2)}, u32[]{:S(2)}) collective-permute-start(bf16[3,192,512]{2,1,0:T(8,128)(2,1)} %bitcast.17), channel_id=1, source_target_pairs={{2,0},{6,4},{3,1},{7,5},{12,14},{8,10},{13,15},{9,11},{18,16},{22,... | collective-permute-start | bytes 1769480 | tf_op jit(solution)/shard_map/cond/branch_0_fun/ppermute | solution.py:215
  190.8 11.3 %branch_0_fun.8 = (bf16[192,1792]{1,0:T(8,128)(2,1)S(1)}, f32[192,1792]{1,0:T(8,128)S(1)}) custom-call(s32[1]{0:T(128)} %bitcast.3.c_ref, bf16[192,1792]{1,0:T(8,128)(2,1)S(1)} %get-tuple-element.80.mine_ref, bf16[192,1792]{1,0:T(8,128)(2,1)S(1)} %collective-permute-done.21.other_ref, bf16[3584,3584]{1,0:T(8,128)(2,1)} %get-tuple-element.226.b_mine_ref.b_other_ref, ...), custom_call_target="tpu_custom_call" | custom-call | flops 1 | bytes 1 | tf_op jit(solution)/shard_map/cond/branch_0_fun/pallas_call | solution.py:74
  208.2 3.0 broadcast_select_fusion.6
  213.0 6.3 %collective-permute-start.29 = (bf16[192,1792]{1,0:T(8,128)(2,1)}, bf16[192,1792]{1,0:T(8,128)(2,1)}, u32[]{:S(2)}, u32[]{:S(2)}) collective-permute-start(bf16[192,1792]{1,0:T(8,128)(2,1)} %get-tuple-element.274), channel_id=1, source_target_pairs={{0,2},{1,3},{2,0},{3,1},{4,6},{5,7},{6,4},{7,5},{8,10},{9,11},{10,... | collective-permute-start | bytes 2064392 | tf_op jit(solution)/shard_map/cond/branch_0_fun/ppermute | solution.py:148
  230.9 11.3 %branch_0_fun.7 = (bf16[192,1792]{1,0:T(8,128)(2,1)S(1)}, f32[192,1792]{1,0:T(8,128)S(1)}) custom-call(s32[1]{0:T(128)} %bitcast.3.c_ref, bf16[192,1792]{1,0:T(8,128)(2,1)S(1)} %broadcast_select_fusion.7.mine_ref, bf16[192,1792]{1,0:T(8,128)(2,1)S(1)} %collective-permute-done.24.other_ref, bf16[3584,3584]{1,0:T(8,128)(2,1)} %get-tuple-element.226.b_mine_ref.b_other_ref, ...), custom_call_target="tpu_custom_call" | custom-call | flops 1 | bytes 1 | tf_op jit(solution)/shard_map/cond/branch_0_fun/pallas_call | solution.py:74
  244.8 6.0 %collective-permute-done.36 = bf16[768,512]{1,0:T(8,128)(2,1)S(1)} collective-permute-done((bf16[768,512]{1,0:T(8,128)(2,1)}, bf16[768,512]{1,0:T(8,128)(2,1)S(1)}, u32[]{:S(2)}, u32[]{:S(2)}) %collective-permute-start.36) | collective-permute-done | bytes 786464 | tf_op jit(solution)/shard_map/cond/branch_0_fun/ppermute | solution.py:215
  254.3 15.9 %collective-permute-done.37 = bf16[768,512]{1,0:T(8,128)(2,1)S(1)} collective-permute-done((bf16[768,512]{1,0:T(8,128)(2,1)S(1)}, bf16[768,512]{1,0:T(8,128)(2,1)S(1)}, u32[]{:S(2)}, u32[]{:S(2)}) %collective-permute-start.37) | collective-permute-done | bytes 786464 | tf_op jit(solution)/shard_map/cond/branch_0_fun/ppermute | solution.py:215
  272.2 2.4 collective-permute-start.39
  280.9 19.1 %branch_0_fun.9 = bf16[3584,1024]{1,0:T(8,128)(2,1)} custom-call(s32[4]{0:T(128)S(1)} %pad_add_fusion.4.start_ref, s32[1]{0:T(128)} %bitcast.3.c_ref, bf16[2,192,1792]{2,1,0:T(8,128)(2,1)S(1)} %pad_maximum_fusion.1.refs_0_, bf16[2,192,1792]{2,1,0:T(8,128)(2,1)S(1)} %pad_maximum_fusion.2.refs_1_, bf16[2,192,1792]{2,1,0:T(8,128)(2,1)S(1)} %collective-permute-done.31.refs_2_, ...), custom_call_target="tpu_custom_call" | custom-call | flops 1 | bytes 1 | tf_op jit(solution)/shard_map/cond/branch_0_fun/pallas_call | solution.py:130
  (164 shorter events, 75.6 us)
Async XLA Ops:
  27.5 18.3 %collective-permute-start.2 = (bf16[192,1792]{1,0:T(8,128)(2,1)S(1)}, bf16[192,1792]{1,0:T(8,128)(2,1)}, u32[]{:S(2)}, u32[]{:S(2)}) collective-permute-start(bf16[192,1792]{1,0:T(8,128)(2,1)S(1)} %get-tuple-element.410), channel_id=1, source_target_pairs={{2,0},{6,4},{3,1},{7,5},{12,14},{8,10},{13,15},{9,11},{18,16},{22,... | collective-permute-start | bytes 2064392 | tf_op jit(solution)/shard_map/cond/branch_0_fun/ppermute | solution.py:215
  34.0 25.2 %collective-permute-start.1 = (bf16[192,1792]{1,0:T(8,128)(2,1)}, bf16[192,1792]{1,0:T(8,128)(2,1)S(1)}, u32[]{:S(2)}, u32[]{:S(2)}) collective-permute-start(bf16[192,1792]{1,0:T(8,128)(2,1)} %collective-permute-done), channel_id=1, source_target_pairs={{4,8},{8,12},{5,9},{9,13},{10,6},{6,2},{11,7},{7,3},{20,24},{24,28... | collective-permute-start | bytes 2064392 | tf_op jit(solution)/shard_map/cond/branch_0_fun/ppermute | solution.py:215
  61.9 15.2 %collective-permute-start.3 = (bf16[192,1792]{1,0:T(8,128)(2,1)S(1)}, bf16[192,1792]{1,0:T(8,128)(2,1)S(1)}, u32[]{:S(2)}, u32[]{:S(2)}) collective-permute-start(bf16[192,1792]{1,0:T(8,128)(2,1)S(1)} %get-tuple-element.292), channel_id=1, source_target_pairs={{0,4},{4,8},{8,12},{1,5},{5,9},{9,13},{14,10},{10,6},{6,2},{15,11}... | collective-permute-start | bytes 2064392 | tf_op jit(solution)/shard_map/cond/branch_0_fun/ppermute | solution.py:215
  63.1 15.8 %collective-permute-start.7 = (bf16[192,1792]{1,0:T(8,128)(2,1)}, bf16[192,1792]{1,0:T(8,128)(2,1)}, u32[]{:S(2)}, u32[]{:S(2)}) collective-permute-start(bf16[192,1792]{1,0:T(8,128)(2,1)} %get-tuple-element.66), channel_id=1, source_target_pairs={{2,0},{6,4},{3,1},{7,5},{12,14},{8,10},{13,15},{9,11},{18,16},{22,... | collective-permute-start | bytes 2064392 | tf_op jit(solution)/shard_map/cond/branch_0_fun/ppermute | solution.py:215
  68.7 14.4 %collective-permute-start.4 = (bf16[192,1792]{1,0:T(8,128)(2,1)}, bf16[192,1792]{1,0:T(8,128)(2,1)}, u32[]{:S(2)}, u32[]{:S(2)}) collective-permute-start(bf16[192,1792]{1,0:T(8,128)(2,1)} %get-tuple-element.67), channel_id=1, source_target_pairs={{4,0},{5,1},{10,14},{11,15},{20,16},{21,17},{26,30},{27,31}} | collective-permute-start | bytes 2064392 | tf_op jit(solution)/shard_map/cond/branch_0_fun/ppermute | solution.py:215
  77.1 14.4 %collective-permute-start.9 = (bf16[192,1792]{1,0:T(8,128)(2,1)S(1)}, bf16[192,1792]{1,0:T(8,128)(2,1)}, u32[]{:S(2)}, u32[]{:S(2)}) collective-permute-start(bf16[192,1792]{1,0:T(8,128)(2,1)S(1)} %collective-permute-done.3), channel_id=1, source_target_pairs={{4,8},{8,12},{5,9},{9,13},{10,6},{6,2},{11,7},{7,3},{20,24},{24,28... | collective-permute-start | bytes 2064392 | tf_op jit(solution)/shard_map/cond/branch_0_fun/ppermute | solution.py:215
  79.0 22.9 %collective-permute-start.8 = (bf16[192,1792]{1,0:T(8,128)(2,1)}, bf16[192,1792]{1,0:T(8,128)(2,1)S(1)}, u32[]{:S(2)}, u32[]{:S(2)}) collective-permute-start(bf16[192,1792]{1,0:T(8,128)(2,1)} %get-tuple-element.67), channel_id=1, source_target_pairs={{2,0},{6,4},{3,1},{7,5},{12,14},{8,10},{13,15},{9,11},{18,16},{22,... | collective-permute-start | bytes 2064392 | tf_op jit(solution)/shard_map/cond/branch_0_fun/ppermute | solution.py:215
  94.3 13.5 %collective-permute-start.10 = (bf16[192,1792]{1,0:T(8,128)(2,1)S(1)}, bf16[192,1792]{1,0:T(8,128)(2,1)S(1)}, u32[]{:S(2)}, u32[]{:S(2)}) collective-permute-start(bf16[192,1792]{1,0:T(8,128)(2,1)S(1)} %get-tuple-element.285), channel_id=1, source_target_pairs={{0,4},{4,8},{8,12},{1,5},{5,9},{9,13},{14,10},{10,6},{6,2},{15,11}... | collective-permute-start | bytes 2064392 | tf_op jit(solution)/shard_map/cond/branch_0_fun/ppermute | solution.py:215
  95.6 12.2 %collective-permute-start.5 = (bf16[192,1792]{1,0:T(8,128)(2,1)S(1)}, bf16[192,1792]{1,0:T(8,128)(2,1)S(1)}, u32[]{:S(2)}, u32[]{:S(2)}) collective-permute-start(bf16[192,1792]{1,0:T(8,128)(2,1)S(1)} %get-tuple-element.406), channel_id=1, source_target_pairs={{0,1},{1,0},{2,3},{3,2},{4,5},{5,4},{6,7},{7,6},{8,9},{9,8},{10,11... | collective-permute-start | bytes 2064392 | tf_op jit(solution)/shard_map/cond/branch_0_fun/ppermute | solution.py:148
  101.7 32.2 %collective-permute-start.15 = (bf16[1024,1024]{1,0:T(8,128)(2,1)}, bf16[1024,1024]{1,0:T(8,128)(2,1)}, u32[]{:S(2)}, u32[]{:S(2)}) collective-permute-start(bf16[1024,1024]{1,0:T(8,128)(2,1)} %get-tuple-element.73), channel_id=1, source_target_pairs={{0,1},{1,0},{2,3},{3,2},{4,5},{5,4},{6,7},{7,6},{8,9},{9,8},{10,11... | collective-permute-start | bytes 6291464 | tf_op jit(solution)/shard_map/cond/branch_0_fun/ppermute | solution.py:148
  101.8 48.9 %collective-permute-start.16 = (bf16[1024,1024]{1,0:T(8,128)(2,1)}, bf16[1024,1024]{1,0:T(8,128)(2,1)}, u32[]{:S(2)}, u32[]{:S(2)}) collective-permute-start(bf16[1024,1024]{1,0:T(8,128)(2,1)} %get-tuple-element.73), channel_id=1, source_target_pairs={{0,2},{1,3},{2,0},{3,1},{4,6},{5,7},{6,4},{7,5},{8,10},{9,11},{10,... | collective-permute-start | bytes 6291464 | tf_op jit(solution)/shard_map/cond/branch_0_fun/ppermute | solution.py:148
  107.8 18.5 %collective-permute-start.11 = (bf16[192,1792]{1,0:T(8,128)(2,1)S(1)}, bf16[192,1792]{1,0:T(8,128)(2,1)S(1)}, u32[]{:S(2)}, u32[]{:S(2)}) collective-permute-start(bf16[192,1792]{1,0:T(8,128)(2,1)S(1)} %collective-permute-done.10), channel_id=1, source_target_pairs={{4,8},{8,12},{5,9},{9,13},{10,6},{6,2},{11,7},{7,3},{20,24},{24,28... | collective-permute-start | bytes 2064392 | tf_op jit(solution)/shard_map/cond/branch_0_fun/ppermute | solution.py:215
  113.4 38.8 %collective-permute-start.13 = (bf16[192,1792]{1,0:T(8,128)(2,1)S(1)}, bf16[192,1792]{1,0:T(8,128)(2,1)S(1)}, u32[]{:S(2)}, u32[]{:S(2)}) collective-permute-start(bf16[192,1792]{1,0:T(8,128)(2,1)S(1)} %copy-done.25), channel_id=1, source_target_pairs={{4,0},{5,1},{10,14},{11,15},{20,16},{21,17},{26,30},{27,31}} | collective-permute-start | bytes 2064392 | tf_op jit(solution)/shard_map/cond/branch_0_fun/ppermute | solution.py:215
  114.1 38.1 %collective-permute-start.20 = (bf16[192,1792]{1,0:T(8,128)(2,1)S(1)}, bf16[192,1792]{1,0:T(8,128)(2,1)S(1)}, u32[]{:S(2)}, u32[]{:S(2)}) collective-permute-start(bf16[192,1792]{1,0:T(8,128)(2,1)S(1)} %copy-done.28), channel_id=1, source_target_pairs={{4,0},{5,1},{10,14},{11,15},{20,16},{21,17},{26,30},{27,31}} | collective-permute-start | bytes 2064392 | tf_op jit(solution)/shard_map/cond/branch_0_fun/ppermute | solution.py:215
  133.9 20.2 %collective-permute-start.12 = (bf16[192,1792]{1,0:T(8,128)(2,1)S(1)}, bf16[192,1792]{1,0:T(8,128)(2,1)}, u32[]{:S(2)}, u32[]{:S(2)}) collective-permute-start(bf16[192,1792]{1,0:T(8,128)(2,1)S(1)} %broadcast_select_fusion.2), channel_id=1, source_target_pairs={{0,4},{4,8},{8,12},{1,5},{5,9},{9,13},{14,10},{10,6},{6,2},{15,11}... | collective-permute-start | bytes 2064392 | tf_op jit(solution)/shard_map/cond/branch_0_fun/ppermute | solution.py:215
  139.1 47.5 %collective-permute-start.19 = (bf16[192,1792]{1,0:T(8,128)(2,1)}, bf16[192,1792]{1,0:T(8,128)(2,1)}, u32[]{:S(2)}, u32[]{:S(2)}) collective-permute-start(bf16[192,1792]{1,0:T(8,128)(2,1)} %get-tuple-element.287), channel_id=1, source_target_pairs={{0,2},{1,3},{2,0},{3,1},{4,6},{5,7},{6,4},{7,5},{8,10},{9,11},{10,... | collective-permute-start | bytes 2064392 | tf_op jit(solution)/shard_map/cond/branch_0_fun/ppermute | solution.py:148
  156.9 30.5 %collective-permute-start.21 = (bf16[192,1792]{1,0:T(8,128)(2,1)}, bf16[192,1792]{1,0:T(8,128)(2,1)S(1)}, u32[]{:S(2)}, u32[]{:S(2)}) collective-permute-start(bf16[192,1792]{1,0:T(8,128)(2,1)} %broadcast_select_fusion.8), channel_id=1, source_target_pairs={{0,1},{1,0},{2,3},{3,2},{4,5},{5,4},{6,7},{7,6},{8,9},{9,8},{10,11... | collective-permute-start | bytes 2064392 | tf_op jit(solution)/shard_map/cond/branch_0_fun/ppermute | solution.py:148
  161.6 25.8 %collective-permute-start.18 = (bf16[192,1792]{1,0:T(8,128)(2,1)}, bf16[192,1792]{1,0:T(8,128)(2,1)}, u32[]{:S(2)}, u32[]{:S(2)}) collective-permute-start(bf16[192,1792]{1,0:T(8,128)(2,1)} %collective-permute-done.12), channel_id=1, source_target_pairs={{4,8},{8,12},{5,9},{9,13},{10,6},{6,2},{11,7},{7,3},{20,24},{24,28... | collective-permute-start | bytes 2064392 | tf_op jit(solution)/shard_map/cond/branch_0_fun/ppermute | solution.py:215
  174.4 14.3 %collective-permute-start.27 = (bf16[192,1792]{1,0:T(8,128)(2,1)S(1)}, bf16[192,1792]{1,0:T(8,128)(2,1)}, u32[]{:S(2)}, u32[]{:S(2)}) collective-permute-start(bf16[192,1792]{1,0:T(8,128)(2,1)S(1)} %get-tuple-element.79), channel_id=1, source_target_pairs={{0,1},{1,0},{2,3},{3,2},{4,5},{5,4},{6,7},{7,6},{8,9},{9,8},{10,11... | collective-permute-start | bytes 2064392 | tf_op jit(solution)/shard_map/cond/branch_0_fun/ppermute | solution.py:148
  180.3 22.3 %collective-permute-start.34 = (bf16[3,192,512]{2,1,0:T(8,128)(2,1)}, bf16[3,192,512]{2,1,0:T(8,128)(2,1)}, u32[]{:S(2)}, u32[]{:S(2)}) collective-permute-start(bf16[3,192,512]{2,1,0:T(8,128)(2,1)} %bitcast.17), channel_id=1, source_target_pairs={{2,0},{6,4},{3,1},{7,5},{12,14},{8,10},{13,15},{9,11},{18,16},{22,... | collective-permute-start | bytes 1769480 | tf_op jit(solution)/shard_map/cond/branch_0_fun/ppermute | solution.py:215
  186.7 21.5 %collective-permute-start.23 = (bf16[192,1792]{1,0:T(8,128)(2,1)}, bf16[192,1792]{1,0:T(8,128)(2,1)S(1)}, u32[]{:S(2)}, u32[]{:S(2)}) collective-permute-start(bf16[192,1792]{1,0:T(8,128)(2,1)} %copy-done.23), channel_id=1, source_target_pairs={{4,0},{5,1},{10,14},{11,15},{20,16},{21,17},{26,30},{27,31}} | collective-permute-start | bytes 2064392 | tf_op jit(solution)/shard_map/cond/branch_0_fun/ppermute | solution.py:215
  187.4 20.8 %collective-permute-start.22 = (bf16[192,1792]{1,0:T(8,128)(2,1)}, bf16[192,1792]{1,0:T(8,128)(2,1)S(1)}, u32[]{:S(2)}, u32[]{:S(2)}) collective-permute-start(bf16[192,1792]{1,0:T(8,128)(2,1)} %collective-permute-done.18), channel_id=1, source_target_pairs={{8,12},{9,13},{6,2},{7,3},{24,28},{25,29},{22,18},{23,19}} | collective-permute-start | bytes 2064392 | tf_op jit(solution)/shard_map/cond/branch_0_fun/ppermute | solution.py:215
  190.8 37.6 %collective-permute-start.30 = (bf16[192,1792]{1,0:T(8,128)(2,1)}, bf16[192,1792]{1,0:T(8,128)(2,1)}, u32[]{:S(2)}, u32[]{:S(2)}) collective-permute-start(bf16[192,1792]{1,0:T(8,128)(2,1)} %fusion.19), channel_id=1, source_target_pairs={{0,2},{1,3},{2,0},{3,1},{4,6},{5,7},{6,4},{7,5},{8,10},{9,11},{10,... | collective-permute-start | bytes 2064392 | tf_op jit(solution)/shard_map/cond/branch_0_fun/ppermute | solution.py:148
  206.6 21.8 %collective-permute-start.35 = (bf16[768,512]{1,0:T(8,128)(2,1)}, bf16[768,512]{1,0:T(8,128)(2,1)}, u32[]{:S(2)}, u32[]{:S(2)}) collective-permute-start(bf16[768,512]{1,0:T(8,128)(2,1)} %pad_maximum_fusion.3), channel_id=1, source_target_pairs={{0,4},{4,8},{1,5},{5,9},{14,10},{10,6},{15,11},{11,7},{16,20},{20,... | collective-permute-start | bytes 2359304 | tf_op jit(solution)/shard_map/cond/branch_0_fun/ppermute | solution.py:215
  211.2 19.7 %collective-permute-start.24 = (bf16[192,1792]{1,0:T(8,128)(2,1)}, bf16[192,1792]{1,0:T(8,128)(2,1)S(1)}, u32[]{:S(2)}, u32[]{:S(2)}) collective-permute-start(bf16[192,1792]{1,0:T(8,128)(2,1)} %get-tuple-element.279), channel_id=1, source_target_pairs={{0,1},{1,0},{2,3},{3,2},{4,5},{5,4},{6,7},{7,6},{8,9},{9,8},{10,11... | collective-permute-start | bytes 2064392 | tf_op jit(solution)/shard_map/cond/branch_0_fun/ppermute | solution.py:148
  213.0 29.8 %collective-permute-start.29 = (bf16[192,1792]{1,0:T(8,128)(2,1)}, bf16[192,1792]{1,0:T(8,128)(2,1)}, u32[]{:S(2)}, u32[]{:S(2)}) collective-permute-start(bf16[192,1792]{1,0:T(8,128)(2,1)} %get-tuple-element.274), channel_id=1, source_target_pairs={{0,2},{1,3},{2,0},{3,1},{4,6},{5,7},{6,4},{7,5},{8,10},{9,11},{10,... | collective-permute-start | bytes 2064392 | tf_op jit(solution)/shard_map/cond/branch_0_fun/ppermute | solution.py:148
  227.7 26.7 %collective-permute-start.38 = (bf16[768,512]{1,0:T(8,128)(2,1)}, bf16[768,512]{1,0:T(8,128)(2,1)S(1)}, u32[]{:S(2)}, u32[]{:S(2)}) collective-permute-start(bf16[768,512]{1,0:T(8,128)(2,1)} %pad_maximum_fusion.3), channel_id=1, source_target_pairs={{4,0},{5,1},{10,14},{11,15},{20,16},{21,17},{26,30},{27,31}} | collective-permute-start | bytes 2359304 | tf_op jit(solution)/shard_map/cond/branch_0_fun/ppermute | solution.py:215
  228.4 22.3 %collective-permute-start.36 = (bf16[768,512]{1,0:T(8,128)(2,1)}, bf16[768,512]{1,0:T(8,128)(2,1)S(1)}, u32[]{:S(2)}, u32[]{:S(2)}) collective-permute-start(bf16[768,512]{1,0:T(8,128)(2,1)} %collective-permute-done.35), channel_id=1, source_target_pairs={{4,8},{8,12},{5,9},{9,13},{10,6},{6,2},{11,7},{7,3},{20,24},{24,28... | collective-permute-start | bytes 2359304 | tf_op jit(solution)/shard_map/cond/branch_0_fun/ppermute | solution.py:215
  242.2 11.9 %collective-permute-start.25 = (bf16[192,1792]{1,0:T(8,128)(2,1)S(1)}, bf16[192,1792]{1,0:T(8,128)(2,1)S(1)}, u32[]{:S(2)}, u32[]{:S(2)}) collective-permute-start(bf16[192,1792]{1,0:T(8,128)(2,1)S(1)} %get-tuple-element.78), channel_id=1, source_target_pairs={{0,1},{1,0},{2,3},{3,2},{4,5},{5,4},{6,7},{7,6},{8,9},{9,8},{10,11... | collective-permute-start | bytes 2064392 | tf_op jit(solution)/shard_map/cond/branch_0_fun/ppermute | solution.py:148
  250.7 19.5 %collective-permute-start.37 = (bf16[768,512]{1,0:T(8,128)(2,1)S(1)}, bf16[768,512]{1,0:T(8,128)(2,1)S(1)}, u32[]{:S(2)}, u32[]{:S(2)}) collective-permute-start(bf16[768,512]{1,0:T(8,128)(2,1)S(1)} %collective-permute-done.36), channel_id=1, source_target_pairs={{8,12},{9,13},{6,2},{7,3},{24,28},{25,29},{22,18},{23,19}} | collective-permute-start | bytes 2359304 | tf_op jit(solution)/shard_map/cond/branch_0_fun/ppermute | solution.py:215
  252.6 28.3 %collective-permute-start.32 = (bf16[2,192,1792]{2,1,0:T(8,128)(2,1)S(1)}, bf16[2,192,1792]{2,1,0:T(8,128)(2,1)S(1)}, u32[]{:S(2)}, u32[]{:S(2)}) collective-permute-start(bf16[2,192,1792]{2,1,0:T(8,128)(2,1)S(1)} %pad_maximum_fusion.2.refs_1_), channel_id=1, source_target_pairs={{0,1},{1,0},{2,3},{3,2},{4,5},{5,4},{6,7},{7,6},{8,9},{9,8},{10,11... | collective-permute-start | bytes 4128776 | tf_op jit(solution)/shard_map/cond/branch_0_fun/ppermute | solution.py:148
  254.2 20.4 %collective-permute-start.26 = (bf16[192,1792]{1,0:T(8,128)(2,1)S(1)}, bf16[192,1792]{1,0:T(8,128)(2,1)S(1)}, u32[]{:S(2)}, u32[]{:S(2)}) collective-permute-start(bf16[192,1792]{1,0:T(8,128)(2,1)S(1)} %fusion.18), channel_id=1, source_target_pairs={{0,2},{1,3},{2,0},{3,1},{4,6},{5,7},{6,4},{7,5},{8,10},{9,11},{10,... | collective-permute-start | bytes 2064392 | tf_op jit(solution)/shard_map/cond/branch_0_fun/ppermute | solution.py:148
  (32 other events, 298.3 us)
